TPU v7x, 32 devices: a whole 2x2x4 slice. The times are simulated.
32 devices in a mesh: groups: 2 (over y), space: 8 (over z, x), tm: 2 (over core).
Axes of the slice: x: 2, y: 2, z: 4, core: 2. Of those that a mesh axis runs over, the one named last changes fastest.
Arguments:
- probes: float32 [16, 4096, 128], P(('groups', 'tm'), 'space'), parts along dimension 0, may hold values from -60 to 60
- phi: float32 [16, 4096], P(('groups', 'tm'), 'space'), parts along dimension 0, may hold values from -0.4 to 0.4
- kcols: int32 [32, 3], P('space'), may hold values from 0 to 31, as said below
- kblocks: float32 [32, 3, 128, 128], P('space'), may hold values from -0.25 to 0.85
Outputs:
- solution: float32 [16, 4096, 128], P(('groups', 'tm'), 'space'), parts along dimension 0
- residual: float32 [16, 4096, 128], P(('groups', 'tm'), 'space'), parts along dimension 0
There are 2 independent parts, one for each index of `groups`. A program takes and returns all parts, laid end to end along the dimension named above; an argument that names none is the same for every part. Nothing has to cross between parts.
Inputs may be any that keep to these rules, and one draw needn't show every extreme that they name: `kcols`: block row i lists block i first, then two distinct other blocks, each within 2 blocks of i.
All inputs are finite; a program needn't handle non-finite values.
Results may differ from a plain program's by a relative error of at most 0.00013.
Values sent between devices are 32-bit elements; how exact they have to be, the bound alone decides.
A program may use at most 64 MiB of HBM per device.

v0:
```python
import jax
import jax.numpy as jnp
from jax import lax
from jax.sharding import PartitionSpec as P

ITERS = 2
REACH = 2


def shifted(block, axis, distance):
    devices = range(lax.axis_size(axis))
    route = [((i - distance) % len(devices), i) for i in devices]
    return lax.ppermute(block, axis, route)


def padded(x, sides, width):
    for axis, dim in sides:
        size, length = (lax.axis_size(axis), x.shape[dim])
        up = [(i, (i + 1) % size) for i in range(size - 1)]
        down = [(j, i) for i, j in up]
        last = lax.slice_in_dim(x, length - width, length, axis=dim)
        initial = lax.slice_in_dim(x, 0, width, axis=dim)
        before = lax.ppermute(last, axis, up)
        after = lax.ppermute(initial, axis, down)
        x = jnp.concatenate([before, x, after], axis=dim)
    return x


def from_behind(block, axis, distance):
    devices = range(lax.axis_size(axis))
    route = [(i - distance, i) for i in devices if i - distance in devices]
    return lax.ppermute(block, axis, route)


def column_sums(left, right):
    return jnp.sum(left * right, axis=(0, 1))


def local(probes, phi, kcols, kblocks):
    slice_count, site_rows, probe_cols = probes.shape
    block_size = kblocks.shape[2]
    own_blocks = kcols.shape[0]
    reach_blocks = REACH
    wide_count = own_blocks + 2 * reach_blocks
    rim_rows = reach_blocks * block_size
    highest = lax.Precision.HIGHEST
    field = jnp.exp(phi)[:, :, None]
    first_dev = lax.axis_index("tm") == 0
    final_dev = lax.axis_index("tm") == lax.axis_size("tm") - 1
    space_pos = lax.axis_index("space")
    local_cols = kcols - (space_pos * own_blocks - reach_blocks)
    spread_onehot = (
        local_cols.reshape(-1)[:, None] == jnp.arange(wide_count, dtype=jnp.int32)[None, :]
    ).astype(jnp.float32)

    def squares(vector):
        return lax.psum(column_sums(vector, vector), ("space", "tm"))

    solution = jnp.zeros_like(probes)
    residual = probes
    direction = probes
    norm_now = squares(residual)
    for iteration in range(ITERS):
        forward_arrived = shifted(direction[-1], "tm", 1)
        forward_arrived = jnp.where(first_dev, -forward_arrived, forward_arrived)
        earlier = jnp.concatenate([forward_arrived[None], direction[:-1]], axis=0)
        forward_spread = padded(field * earlier, (("space", 1),), rim_rows)
        forward_pieces = forward_spread.reshape(slice_count, wide_count, block_size, probe_cols)
        picked = jnp.take(forward_pieces, local_cols, axis=1)
        moved = jnp.einsum("nkab,snkbp->snap", kblocks, picked, precision=highest)
        image = direction - moved.reshape(slice_count, site_rows, probe_cols)
        alpha = norm_now / lax.psum(column_sums(image, image), ("space", "tm"))
        solution = solution + alpha * direction
        pieces = image.reshape(slice_count, own_blocks, block_size, probe_cols)
        terms = jnp.einsum("nkba,snbp->snkap", kblocks, pieces, precision=highest)
        terms = terms.reshape(slice_count, -1, block_size, probe_cols)
        spread = jnp.einsum("cm,scap->smap", spread_onehot, terms, precision=highest)
        from_next = from_behind(spread[:, :reach_blocks], "space", -1)
        from_prev = from_behind(spread[:, reach_blocks + own_blocks :], "space", 1)
        summed = spread[:, reach_blocks : reach_blocks + own_blocks]
        summed = summed.at[:, own_blocks - reach_blocks :].add(from_next)
        summed = summed.at[:, :reach_blocks].add(from_prev)
        scaled = field * summed.reshape(slice_count, site_rows, probe_cols)
        arrived = shifted(scaled[0], "tm", -1)
        arrived = jnp.where(final_dev, -arrived, arrived)
        later = jnp.concatenate([scaled[1:], arrived[None]], axis=0)
        residual = residual - alpha * (image - later)
        norm_next = squares(residual)
        direction = residual + norm_next / norm_now * direction
        norm_now = norm_next
    return (solution, residual)


def solution(mesh):
    placed = (
        P(("groups", "tm"), "space", None),
        P(("groups", "tm"), "space"),
        P("space", None),
        P("space", None, None, None),
    )
    return jax.shard_map(
        local,
        mesh=mesh,
        in_specs=placed,
        out_specs=(P(("groups", "tm"), "space", None), P(("groups", "tm"), "space", None)),
        check_vma=False,
    )
```

profile of v0, /device:TPU:0, one launch (start us, length us, event | category | flops | bytes accessed | tf_op | source)
XLA Modules:
  0.0 268.2 jit_solution(8138009165283746609)
XLA Ops:
  0.7 1.1 slice_bitcast_fusion.3
  1.7 0.5 collective-permute-start
  2.3 0.7 exp.3
  3.0 0.4 collective-permute-done
  3.8 1.0 copy-done.3
  4.8 4.8 %collective-permute-start.1 = (f32[4,256,128]{2,1,0:T(8,128)S(1)}, f32[4,256,128]{2,1,0:T(8,128)S(1)}, u32[]{:S(2)}, u32[]{:S(2)}) collective-permute-start(f32[4,256,128]{2,1,0:T(8,128)S(1)} %get-tuple-element.68), channel_id=1, source_target_pairs={{0,2},{2,4},{4,6},{6,8},{8,10},{10,12},{12,14},{1,3},{3,5},{5,7},{... | collective-permute-start | bytes 1572872 | tf_op jit(solution)/shard_map/ppermute | solution.py:23
  9.6 1.3 collective-permute-start.2
  11.2 21.2 %collective-permute-done.1 = f32[4,256,128]{2,1,0:T(8,128)S(1)} collective-permute-done((f32[4,256,128]{2,1,0:T(8,128)S(1)}, f32[4,256,128]{2,1,0:T(8,128)S(1)}, u32[]{:S(2)}, u32[]{:S(2)}) %collective-permute-start.1) | collective-permute-done | bytes 524320 | tf_op jit(solution)/shard_map/ppermute | solution.py:23
  32.3 1.5 pad_maximum_fusion
  33.9 2.4 gather_fusion
  36.3 4.4 %fusion.20 = f32[4,4,128,128]{3,2,0,1:T(8,128)S(1)} fusion(f32[4,3,4,128,128]{4,3,2,1,0:T(8,128)} %bitcast.95, pred[4,3]{1,0:T(4,128)(4,1)S(1)} %get-tuple-element.59, f32[4,3,128,128]{3,2,1,0:T(8,128)S(1)} %copy-done), kind=kOutput, calls=%fused_computation.22 | convolution fusion | flops 1208745984 | bytes 4980748 | tf_op jit(solution)/shard_map/nkab,snkbp->snap/dot_general | solution.py:70
  41.1 4.3 %convolution_bitcast_fusion.1 = f32[4,4,3,128,128]{3,4,2,0,1:T(8,128)} fusion(f32[4,4,128,128,1]{3,2,1,0,4:T(8,128)S(1)} %bitcast.96, f32[4,3,128,128]{3,2,1,0:T(8,128)S(1)} %copy-done), kind=kOutput, calls=%fused_computation.15 | convolution fusion | flops 1207959552 | bytes 4980736 | tf_op jit(solution)/shard_map/nkba,snbp->snkap/dot_general | solution.py:75
  45.4 3.6 %copy.11 = f32[4,4,3,128,128]{4,3,2,1,0:T(8,128)} copy(f32[4,4,3,128,128]{3,4,2,0,1:T(8,128)} %convolution_bitcast_fusion.1) | data formatting | bytes 6291456 | tf_op jit(solution)/shard_map/nkba,snbp->snkap/transpose | solution.py:75
  48.9 6.1 %fusion.10 = f32[4,8,128,128]{3,1,2,0:T(8,128)S(1)} fusion(f32[4,12,128,128]{3,2,1,0:T(8,128)} %bitcast.91, s32[12]{0:T(128)S(1)} %eq.22), kind=kOutput, calls=%fused_computation.16 | convolution fusion | flops 75497568 | bytes 5242928 | tf_op jit(solution)/shard_map/cm,scap->smap/dot_general | solution.py:77
  55.3 1.3 collective-permute-start.3
  56.6 5.2 %collective-permute-start.4 = (f32[4,2,128,128]{3,1,2,0:T(2,128)S(1)}, f32[4,2,128,128]{3,1,2,0:T(2,128)S(1)}, u32[]{:S(2)}, u32[]{:S(2)}) collective-permute-start(f32[4,2,128,128]{3,1,2,0:T(2,128)S(1)} %get-tuple-element.63), channel_id=1, source_target_pairs={{0,2},{2,4},{4,6},{6,8},{8,10},{10,12},{12,14},{1,3},{3,5},{5,7},{... | collective-permute-start | bytes 1572872 | tf_op jit(solution)/shard_map/ppermute | solution.py:32
  62.1 9.0 %collective-permute-done.3 = f32[4,2,128,128]{3,1,2,0:T(2,128)S(1)} collective-permute-done((f32[4,2,128,128]{3,1,2,0:T(2,128)S(1)}, f32[4,2,128,128]{3,1,2,0:T(2,128)S(1)}, u32[]{:S(2)}, u32[]{:S(2)}) %collective-permute-start.3) | collective-permute-done | bytes 524320 | tf_op jit(solution)/shard_map/ppermute | solution.py:32
  71.1 0.5 fusion.39
  71.7 11.5 %collective-permute-done.4 = f32[4,2,128,128]{3,1,2,0:T(2,128)S(1)} collective-permute-done((f32[4,2,128,128]{3,1,2,0:T(2,128)S(1)}, f32[4,2,128,128]{3,1,2,0:T(2,128)S(1)}, u32[]{:S(2)}, u32[]{:S(2)}) %collective-permute-start.4) | collective-permute-done | bytes 524320 | tf_op jit(solution)/shard_map/ppermute | solution.py:32
  83.1 0.5 fusion.38
  83.7 0.3 bitcast_multiply_fusion.1
  84.1 1.0 copy-done.4
  85.1 33.9 %all-reduce = (f32[128]{0:T(128)S(1)}, f32[128]{0:T(128)S(1)}) all-reduce(f32[128]{0:T(128)S(1)} %get-tuple-element.67, f32[128]{0:T(128)S(1)} %get-tuple-element.57), channel_id=1, replica_groups=mesh['groups'=2,'space'=8,'tm'=2] {'space','tm'}, use_global_device_ids=true, to_apply=%region_1.0 | all-reduce | flops 256 | bytes 2048 | tf_op jit(solution)/shard_map/psum | solution.py:57
  119.0 1.2 slice.205
  120.3 1.3 multiply_reduce_fusion.1
  121.5 29.5 %psum.30 = f32[128]{0:T(128)S(1)} all-reduce(f32[128]{0:T(128)S(1)} %get-tuple-element.55), channel_id=1, replica_groups=mesh['groups'=2,'space'=8,'tm'=2] {'space','tm'}, use_global_device_ids=true, to_apply=%region_5.7 | all-reduce | flops 128 | bytes 1024 | tf_op jit(solution)/shard_map/psum | solution.py:57
  151.0 1.3 multiply_add_fusion.1
  152.5 1.5 collective-permute-done.6
  154.4 1.3 collective-permute-start.7
  155.7 1.3 collective-permute-start.8
  157.0 21.6 %collective-permute-done.7 = f32[4,256,128]{2,1,0:T(8,128)S(1)} collective-permute-done((f32[4,256,128]{2,1,0:T(8,128)S(1)}, f32[4,256,128]{2,1,0:T(8,128)S(1)}, u32[]{:S(2)}, u32[]{:S(2)}) %collective-permute-start.7) | collective-permute-done | bytes 524320 | tf_op jit(solution)/shard_map/ppermute | solution.py:23
  178.7 1.5 pad_maximum_fusion.1
  180.2 4.0 %gather_fusion.1 = f32[12,4,128,128]{3,2,1,0:T(8,128)} fusion(f32[4,8,128,128]{3,2,1,0:T(8,128)} %bitcast.92, s32[1024]{0:T(1024)S(1)} %pad_clamp_fusion), kind=kCustom, calls=%fused_computation.1.clone | custom fusion | bytes 6291504 | tf_op jit(solution)/shard_map/jit(_take)/gather | solution.py:69
  184.1 4.3 %fusion.23 = f32[4,4,128,128]{3,2,0,1:T(8,128)S(1)} fusion(f32[4,3,4,128,128]{4,3,2,1,0:T(8,128)} %bitcast.94, pred[4,3]{1,0:T(4,128)(4,1)S(1)} %get-tuple-element.59, f32[4,3,128,128]{3,2,1,0:T(8,128)S(1)} %copy-done), kind=kOutput, calls=%fused_computation.23 | convolution fusion | flops 1208745984 | bytes 4980748 | tf_op jit(solution)/shard_map/nkab,snkbp->snap/dot_general | solution.py:70
  188.9 1.0 copy-done.2
  189.8 4.4 %convolution_bitcast_fusion = f32[4,4,3,128,128]{3,4,2,0,1:T(8,128)} fusion(f32[4,4,128,128,1]{3,2,1,0,4:T(8,128)S(1)} %bitcast.97, f32[4,3,128,128]{3,2,1,0:T(8,128)S(1)} %copy-done), kind=kOutput, calls=%fused_computation.14 | convolution fusion | flops 1207959552 | bytes 4980736 | tf_op jit(solution)/shard_map/nkba,snbp->snkap/dot_general | solution.py:75
  194.2 3.6 %copy.17 = f32[4,4,3,128,128]{4,3,2,1,0:T(8,128)} copy(f32[4,4,3,128,128]{3,4,2,0,1:T(8,128)} %convolution_bitcast_fusion) | data formatting | bytes 6291456 | tf_op jit(solution)/shard_map/nkba,snbp->snkap/transpose | solution.py:75
  197.8 6.1 %fusion.13 = f32[4,8,128,128]{3,1,2,0:T(8,128)S(1)} fusion(f32[4,12,128,128]{3,2,1,0:T(8,128)} %bitcast.90, s32[12]{0:T(128)S(1)} %eq.22), kind=kOutput, calls=%fused_computation.17 | convolution fusion | flops 75497568 | bytes 5242928 | tf_op jit(solution)/shard_map/cm,scap->smap/dot_general | solution.py:77
  204.2 1.3 collective-permute-start.9
  205.5 5.0 %collective-permute-start.10 = (f32[4,2,128,128]{3,1,2,0:T(2,128)S(1)}, f32[4,2,128,128]{3,1,2,0:T(2,128)S(1)}, u32[]{:S(2)}, u32[]{:S(2)}) collective-permute-start(f32[4,2,128,128]{3,1,2,0:T(2,128)S(1)} %get-tuple-element.61), channel_id=1, source_target_pairs={{0,2},{2,4},{4,6},{6,8},{8,10},{10,12},{12,14},{1,3},{3,5},{5,7},{... | collective-permute-start | bytes 1572872 | tf_op jit(solution)/shard_map/ppermute | solution.py:32
  210.8 9.7 %collective-permute-done.9 = f32[4,2,128,128]{3,1,2,0:T(2,128)S(1)} collective-permute-done((f32[4,2,128,128]{3,1,2,0:T(2,128)S(1)}, f32[4,2,128,128]{3,1,2,0:T(2,128)S(1)}, u32[]{:S(2)}, u32[]{:S(2)}) %collective-permute-start.9) | collective-permute-done | bytes 524320 | tf_op jit(solution)/shard_map/ppermute | solution.py:32
  220.5 0.5 fusion.37
  221.0 10.8 %collective-permute-done.10 = f32[4,2,128,128]{3,1,2,0:T(2,128)S(1)} collective-permute-done((f32[4,2,128,128]{3,1,2,0:T(2,128)S(1)}, f32[4,2,128,128]{3,1,2,0:T(2,128)S(1)}, u32[]{:S(2)}, u32[]{:S(2)}) %collective-permute-start.10) | collective-permute-done | bytes 524320 | tf_op jit(solution)/shard_map/ppermute | solution.py:32
  231.8 0.5 fusion.36
  232.8 1.0 copy-done.5
  233.8 30.0 %psum.31 = f32[128]{0:T(128)S(1)} all-reduce(f32[128]{0:T(128)S(1)} %get-tuple-element.53), channel_id=1, replica_groups=mesh['groups'=2,'space'=8,'tm'=2] {'space','tm'}, use_global_device_ids=true, to_apply=%region_7.9 | all-reduce | flops 128 | bytes 1024 | tf_op jit(solution)/shard_map/psum | solution.py:72
  263.8 1.2 slice.216
  265.0 3.2 %fusion.29 = (f32[4,512,128]{2,1,0:T(8,128)}, f32[4,512,128]{2,1,0:T(8,128)}) fusion(f32[4,512,128]{2,1,0:T(8,128)} %get-tuple-element.56, f32[4,512,128]{2,1,0:T(8,128)} %copy-done.2, f32[1,512,128]{2,1,0:T(8,128)S(1)} %fusion.43, f32[3,512,128]{2,1,0:T(8,128)S(1)} %slice.216, f32[128]{0:T(128)S(1)} %div.11, f32[4,512,128]{2,1,0:T(8,128)S(1)} %multiply_add_fusion.1, ...), kind=kLoop, calls=%fused_computation.31 | loop fusion | flops 1835008 | bytes 7341056 | tf_op jit(solution)/shard_map/sub | solution.py:87
  (50 shorter events, 3.9 us)
Async XLA Ops:
  0.6 35.6 %copy-start = (f32[4,3,128,128]{3,2,1,0:T(8,128)S(1)}, f32[4,3,128,128]{3,2,1,0:T(8,128)}, u32[]{:S(2)}) copy-start(f32[4,3,128,128]{3,2,1,0:T(8,128)} %param.17) | copy-start | bytes 2359300
  0.6 2.8 %slice-start = ((f32[4,512,128]{2,1,0:T(8,128)}), f32[3,512,128]{2,1,0:T(8,128)S(1)}, s32[]{:S(2)}) async-start(f32[4,512,128]{2,1,0:T(8,128)} %param.14), calls=%async_computation | async-start | bytes 1572864 | tf_op jit(solution)/shard_map/slice | solution.py:66
  1.7 1.7 collective-permute-start
  2.3 8.7 %copy-start.6 = (s32[4,3]{1,0:T(4,128)S(1)}, s32[4,3]{1,0:T(4,128)}, u32[]{:S(2)}) copy-start(s32[4,3]{1,0:T(4,128)} %param.16) | copy-start | bytes 148
  3.8 1.0 copy-start.3
  4.8 27.5 %collective-permute-start.1 = (f32[4,256,128]{2,1,0:T(8,128)S(1)}, f32[4,256,128]{2,1,0:T(8,128)S(1)}, u32[]{:S(2)}, u32[]{:S(2)}) collective-permute-start(f32[4,256,128]{2,1,0:T(8,128)S(1)} %get-tuple-element.68), channel_id=1, source_target_pairs={{0,2},{2,4},{4,6},{6,8},{8,10},{10,12},{12,14},{1,3},{3,5},{5,7},{... | collective-permute-start | bytes 1572872 | tf_op jit(solution)/shard_map/ppermute | solution.py:23
  9.6 22.7 %collective-permute-start.2 = (f32[4,256,128]{2,1,0:T(8,128)S(1)}, f32[4,256,128]{2,1,0:T(8,128)}, u32[]{:S(2)}, u32[]{:S(2)}) collective-permute-start(f32[4,256,128]{2,1,0:T(8,128)S(1)} %get-tuple-element.69), channel_id=1, source_target_pairs={{2,0},{4,2},{6,4},{8,6},{10,8},{12,10},{14,12},{3,1},{5,3},{7,5},{... | collective-permute-start | bytes 1572872 | tf_op jit(solution)/shard_map/ppermute | solution.py:24
  36.2 4.5 %copy-start.1 = (f32[4,512,128]{2,1,0:T(8,128)S(1)}, f32[4,512,128]{2,1,0:T(8,128)}, u32[]{:S(2)}) copy-start(f32[4,512,128]{2,1,0:T(8,128)} %param.14) | copy-start | bytes 3145732
  55.3 15.8 %collective-permute-start.3 = (f32[4,2,128,128]{3,1,2,0:T(2,128)S(1)}, f32[4,2,128,128]{3,1,2,0:T(2,128)S(1)}, u32[]{:S(2)}, u32[]{:S(2)}) collective-permute-start(f32[4,2,128,128]{3,1,2,0:T(2,128)S(1)} %get-tuple-element.64), channel_id=1, source_target_pairs={{2,0},{4,2},{6,4},{8,6},{10,8},{12,10},{14,12},{3,1},{5,3},{7,5},{... | collective-permute-start | bytes 1572872 | tf_op jit(solution)/shard_map/ppermute | solution.py:32
  56.6 26.5 %collective-permute-start.4 = (f32[4,2,128,128]{3,1,2,0:T(2,128)S(1)}, f32[4,2,128,128]{3,1,2,0:T(2,128)S(1)}, u32[]{:S(2)}, u32[]{:S(2)}) collective-permute-start(f32[4,2,128,128]{3,1,2,0:T(2,128)S(1)} %get-tuple-element.63), channel_id=1, source_target_pairs={{0,2},{2,4},{4,6},{6,8},{8,10},{10,12},{12,14},{1,3},{3,5},{5,7},{... | collective-permute-start | bytes 1572872 | tf_op jit(solution)/shard_map/ppermute | solution.py:32
  84.1 1.0 copy-start.4
  85.1 35.2 %collective-permute-start.5 = (f32[512,128]{1,0:T(8,128)S(1)}, f32[512,128]{1,0:T(8,128)S(1)}, u32[]{:S(2)}, u32[]{:S(2)}) collective-permute-start(f32[512,128]{1,0:T(8,128)S(1)} %slice_bitcast_fusion.2), channel_id=1, source_target_pairs={{1,0},{0,1},{3,2},{2,3},{5,4},{4,5},{7,6},{6,7},{9,8},{8,9},{11,10... | collective-permute-start | bytes 786440 | tf_op jit(solution)/shard_map/ppermute | solution.py:13
  152.4 1.6 collective-permute-start.6
  154.4 24.3 %collective-permute-start.7 = (f32[4,256,128]{2,1,0:T(8,128)S(1)}, f32[4,256,128]{2,1,0:T(8,128)S(1)}, u32[]{:S(2)}, u32[]{:S(2)}) collective-permute-start(f32[4,256,128]{2,1,0:T(8,128)S(1)} %get-tuple-element.65), channel_id=1, source_target_pairs={{0,2},{2,4},{4,6},{6,8},{8,10},{10,12},{12,14},{1,3},{3,5},{5,7},{... | collective-permute-start | bytes 1572872 | tf_op jit(solution)/shard_map/ppermute | solution.py:23
  155.7 23.0 %collective-permute-start.8 = (f32[4,256,128]{2,1,0:T(8,128)S(1)}, f32[4,256,128]{2,1,0:T(8,128)S(1)}, u32[]{:S(2)}, u32[]{:S(2)}) collective-permute-start(f32[4,256,128]{2,1,0:T(8,128)S(1)} %get-tuple-element.66), channel_id=1, source_target_pairs={{2,0},{4,2},{6,4},{8,6},{10,8},{12,10},{14,12},{3,1},{5,3},{7,5},{... | collective-permute-start | bytes 1572872 | tf_op jit(solution)/shard_map/ppermute | solution.py:24
  188.9 1.0 copy-start.2
  204.2 16.3 %collective-permute-start.9 = (f32[4,2,128,128]{3,1,2,0:T(2,128)S(1)}, f32[4,2,128,128]{3,1,2,0:T(2,128)S(1)}, u32[]{:S(2)}, u32[]{:S(2)}) collective-permute-start(f32[4,2,128,128]{3,1,2,0:T(2,128)S(1)} %get-tuple-element.62), channel_id=1, source_target_pairs={{2,0},{4,2},{6,4},{8,6},{10,8},{12,10},{14,12},{3,1},{5,3},{7,5},{... | collective-permute-start | bytes 1572872 | tf_op jit(solution)/shard_map/ppermute | solution.py:32
  205.5 26.3 %collective-permute-start.10 = (f32[4,2,128,128]{3,1,2,0:T(2,128)S(1)}, f32[4,2,128,128]{3,1,2,0:T(2,128)S(1)}, u32[]{:S(2)}, u32[]{:S(2)}) collective-permute-start(f32[4,2,128,128]{3,1,2,0:T(2,128)S(1)} %get-tuple-element.61), channel_id=1, source_target_pairs={{0,2},{2,4},{4,6},{6,8},{8,10},{10,12},{12,14},{1,3},{3,5},{5,7},{... | collective-permute-start | bytes 1572872 | tf_op jit(solution)/shard_map/ppermute | solution.py:32
  232.8 1.0 copy-start.5
  233.8 31.2 %collective-permute-start.11 = (f32[512,128]{1,0:T(8,128)S(1)}, f32[512,128]{1,0:T(8,128)S(1)}, u32[]{:S(2)}, u32[]{:S(2)}) collective-permute-start(f32[512,128]{1,0:T(8,128)S(1)} %slice_bitcast_fusion), channel_id=1, source_target_pairs={{1,0},{0,1},{3,2},{2,3},{5,4},{4,5},{7,6},{6,7},{9,8},{8,9},{11,10... | collective-permute-start | bytes 786440 | tf_op jit(solution)/shard_map/ppermute | solution.py:13
where the time goes:
time: 269 us; the launch traced here: 268 us
  blocking collectives  93.3 us (35%)
  waiting for transfers between devices  85.7 us (32%)
  matrix products  29.6 us (11%)
  local copies, waits for them, and re-layouts  23.4 us (9%)
  starting transfers between devices  22.3 us (8%)
  other arithmetic  12.8 us (5%)
    psum x2, blocking collectives, squares(): return lax.psum(column_sums(vector, vector), ('space', 'tm'))  63.4 us
    ppermute x2, waiting for transfers between devices, padded(): before = lax.ppermute(last, axis, up)  42.8 us
    ppermute x4, waiting for transfers between devices, from_behind(): return lax.ppermute(block, axis, route)  41 us
    psum x1, blocking collectives, local(): alpha = norm_now / lax.psum(column_sums(image, image), ('space', 'tm'))  30 us
    ppermute x4, starting transfers between devices, from_behind(): return lax.ppermute(block, axis, route)  12.9 us
    dot_general x2, matrix products, local(): jnp.einsum('cm,scap->smap', spread_onehot, terms, precision=highest)  12.1 us
    dot_general x2, matrix products, local(): moved = jnp.einsum('nkab,snkbp->snap', kblocks, picked, precision=highest)  8.78 us
    dot_general x2, matrix products, local(): terms = jnp.einsum('nkba,snbp->snkap', kblocks, pieces, precision=highest)  8.71 us
  transfers between devices with their start and end apart: 12, of which 8 were waited for; matrix products, arithmetic and copies ran while one was open for 2% of the time, Pallas kernels for 0%

commit v1 on v0

v1 whole, which is shorter than its diff:
```python
import functools

import jax
import jax.numpy as jnp
from jax import lax
from jax.experimental import pallas as pl
from jax.experimental.pallas import tpu as pltpu
from jax.sharding import PartitionSpec as P

MESH = pl.DeviceIdType.MESH
B = 128
OFFS = (-2, -1, 1, 2)


PX, SMALL, KX, KC, TM, DOWN, UP, R1X, R2X, CX = 0, 1, 2, 3, 4, 8, 12, 16, 17, 18
NSEM = 19


def roll64(x):
    return pltpu.roll(x, 64, axis=1)


def split(x):
    high = x.astype(jnp.bfloat16)
    return high, (x - high.astype(jnp.float32)).astype(jnp.bfloat16)


def dot(a, b):
    return jnp.dot(a, b, preferred_element_type=jnp.float32)


def kernel(
    pairs, x_ref, small_ref, k_ref, sol_ref, res_ref,
    px, d, f, sc1, sc2, im, y, r1, r2, r1p, r2p, yr, tms, tmr, smalls, kraw,
    kh, kl, kth, ktl, vh, vl, redsrc, red, coef, coefp,
    ssem, rsem, redss, redrs, lsem,
):
    g, s, t = lax.axis_index("groups"), lax.axis_index("space"), lax.axis_index("tm")
    p, h = s // 2, s % 2
    o = 1 - h
    team = 2 * pairs
    me = p * 2 + t
    peer = (g, s + 1 - 2 * h, t)
    mate = (g, s, 1 - t)
    below = (g, jnp.maximum(s - 2, 0), t)
    above = (g, jnp.minimum(s + 2, 2 * pairs - 1), t)
    has_below, has_above = p > 0, p < pairs - 1

    def member(index):
        return (g, (index // 2) * 2 + h, index % 2)

    barrier = pltpu.get_barrier_semaphore()

    @pl.loop(0, team - 1)
    def _(i):
        pl.semaphore_signal(
            barrier, inc=1, device_id=member(lax.rem(me + 1 + i, team)), device_id_type=MESH
        )

    pl.semaphore_signal(barrier, inc=1, device_id=peer, device_id_type=MESH)

    lane = lax.broadcasted_iota(jnp.int32, (1, 128), 1)
    left = lane < 64
    is0 = h == 0

    def remote(src, dst, index, device):
        return pltpu.make_async_remote_copy(
            src_ref=src, dst_ref=dst, send_sem=ssem.at[index], recv_sem=rsem.at[index],
            device_id=device, device_id_type=MESH,
        )

    own_rows = pl.ds(pl.multiple_of(h * 512, 512), 512)
    peer_rows = pl.ds(pl.multiple_of(o * 512, 512), 512)
    kown = pltpu.make_async_copy(k_ref, kraw.at[pl.ds(h * 12, 12)], lsem)
    kown.start()

    @pl.loop(0, 4)
    def _(i):
        rows = pl.ds(pl.multiple_of(i * B, B), B)
        mine_rows = pl.ds(pl.multiple_of(h * 512 + i * B, B), B)
        for a in range(2):
            xa, xb = x_ref[a, rows, :], x_ref[a + 2, rows, :]
            low = jnp.where(left, xa, roll64(xb))
            high = jnp.where(left, roll64(xa), xb)
            cols = slice(a * 128, a * 128 + 128)
            px[rows, cols] = jnp.where(is0, high, low)
            d[mine_rows, cols] = jnp.where(is0, low, high)

    smalls[h] = small_ref[...]
    pl.semaphore_wait(barrier, team)

    c_px = remote(px, d.at[own_rows], PX, peer)
    c_px.start()
    c_small = remote(small_ref, smalls.at[h], SMALL, peer)
    c_small.start()
    c_kx = remote(k_ref.at[pl.ds(t * 6, 6)], kraw.at[pl.ds(h * 12 + t * 6, 6)], KX, peer)
    c_kx.start()

    def make_field(half):
        @pl.loop(0, 4)
        def _(j):
            e = jnp.exp(smalls[half, pl.ds(pl.multiple_of(j * 16 + 8, 8), 8), :])
            rows = pl.ds(pl.multiple_of(half * 512 + j * B, B), B)
            top = lax.broadcasted_iota(jnp.int32, (B, 128), 0) < 64
            for a in range(2):
                m = jnp.where(top, e[a : a + 1, :], e[a + 2 : a + 3, :])
                f[rows, a * 128 : a * 128 + 128] = m.T

    def make_bands(half):
        @pl.loop(0, 2)
        def _(jj):
            band = half * 2 + jj
            for ri in range(2):
                j = jj * 2 + ri
                k0, k1, k2 = (kraw[half * 12 + 3 * j + k] for k in range(3))
                t0, t1, t2 = k0.T, k1.T, k2.T
                sel = smalls[half, pl.ds(pl.multiple_of(j * 16, 8), 8), :]
                rr = slice(ri * B, ri * B + B)
                empty = 5 * (1 - ri)
                ec = slice(empty * B, empty * B + B)
                zero = jnp.zeros((B, B), jnp.bfloat16)
                kh[band, rr, ec] = zero
                kl[band, rr, ec] = zero
                kth[band, ec, rr] = zero
                ktl[band, ec, rr] = zero
                for off in range(-2, 3):
                    w = off + 2 + ri
                    wc = slice(w * B, w * B + B)
                    if off == 0:
                        blk, blt = k0, t0
                    else:
                        i1 = OFFS.index(off)
                        s1, s2 = sel[i1 : i1 + 1, :], sel[4 + i1 : 5 + i1, :]
                        blk, blt = s1 * k1 + s2 * k2, s1 * t1 + s2 * t2
                    kh[band, rr, wc], kl[band, rr, wc] = split(blk)
                    kth[band, wc, rr], ktl[band, wc, rr] = split(blt)

    def swap_slices(panel, cols, n, first_half_rolled):
        a, b = panel[0:512, cols], panel[512:1024, cols]
        if first_half_rolled:
            tms[n] = jnp.where(left, roll64(a), b)
        else:
            tms[n] = jnp.where(left, a, roll64(b))
        copy = remote(tms.at[n], tmr.at[n], TM + n, mate)
        copy.start()
        return copy

    def halo(low_src, low_dst, high_src, high_dst, n):
        down = remote(low_src, low_dst, DOWN + n, below)
        up = remote(high_src, high_dst, UP + n, above)

        @pl.when(has_below)
        def _():
            down.start()

        @pl.when(has_above)
        def _():
            up.start()

        return down, up

    def halo_arrived(copies):
        down, up = copies

        @pl.when(has_above)
        def _():
            down.wait_recv()

        @pl.when(has_below)
        def _():
            up.wait_recv()

    def halo_sent(copies):
        down, up = copies

        @pl.when(has_below)
        def _():
            down.wait_send()

        @pl.when(has_above)
        def _():
            up.wait_send()

    def scaled_earlier(panel, out, n, copy):
        copy.wait_recv()
        sign = jnp.where(t == 0, -1.0, 1.0)
        got = tmr[n]
        rolled = roll64(panel[:, 128:256])
        out[256:768, 0:128] = f[0:512, 0:128] * jnp.where(left, sign * got, rolled[0:512])
        out[768:1280, 0:128] = f[512:1024, 0:128] * jnp.where(
            left, sign * roll64(got), rolled[512:1024]
        )
        out[256:1280, 128:256] = f[:, 128:256] * panel[:, 0:128]

    def squares(panel):
        q = panel[...]
        q = jnp.sum((q * q).reshape(128, 8, 256), axis=0)
        q = q[:, 0:128] + q[:, 128:256]
        return q + roll64(q)

    def reduce_start(n):
        @pl.loop(0, team - 1)
        def _(i):
            pltpu.make_async_remote_copy(
                src_ref=redsrc.at[n], dst_ref=red.at[n, team - 2 - i],
                send_sem=redss.at[n], recv_sem=redrs.at[n],
                device_id=member(lax.rem(me + 1 + i, team)), device_id_type=MESH,
            ).start()

    def reduce_done(n):
        pltpu.make_async_copy(red.at[n], red.at[n], redrs.at[n]).wait()
        total = redsrc[n] + jnp.sum(red[n], axis=0)
        return (
            jnp.sum(total[0:8], axis=0, keepdims=True),
            jnp.sum(total[8:16], axis=0, keepdims=True),
        )

    def twice(v):
        return jnp.concatenate([v, v], axis=1)

    def forward():
        @pl.loop(0, 4)
        def _(i):
            win = pl.ds(pl.multiple_of(i * 256, 256), 768)
            rows = pl.ds(pl.multiple_of(i * 256, 256), 256)
            vhi = vh[win, :]
            acc = dot(kh[i], vhi) + dot(kl[i], vhi) + dot(kh[i], vl[win, :])
            im[rows, :] = d[rows, :] - acc

    def back_part(i):
        zh, zl = split(im[pl.ds(pl.multiple_of(i * 256, 256), 256), :])
        return dot(kth[i], zh) + dot(ktl[i], zh) + dot(kth[i], zl)

    def backward(n):
        @pl.loop(0, 2)
        def _(i):
            y[pl.ds(pl.multiple_of(i * 768, 256), 768), :] = back_part(i * 3)

        copies = halo(
            y.at[0:256], yr.at[n, 1], y.at[1280:1536], yr.at[n, 0], 1 + 2 * n
        )

        @pl.loop(1, 3)
        def _(i):
            win = pl.ds(pl.multiple_of(i * 256, 256), 768)
            y[win, :] += back_part(i)

        return copies

    def apply_later(n, copies, source, out, alpha):
        halo_arrived(copies)
        y[256:512, :] = f[0:256, :] * (y[256:512, :] + yr[n, 0])
        y[512:1024, :] = f[256:768, :] * y[512:1024, :]
        y[1024:1280, :] = f[768:1024, :] * (y[1024:1280, :] + yr[n, 1])
        slot = 1 + 2 * n
        copy = swap_slices(y.at[256:1280], slice(0, 128), slot, False)
        a1 = alpha
        out[:, 0:128] = source[:, 0:128] - a1 * (im[:, 0:128] - y[256:1280, 128:256])
        copy.wait_recv()
        sign = jnp.where(t == 1, -1.0, 1.0)
        got = tmr[slot]
        rolled = roll64(y[256:1280, 0:128])
        out[0:512, 128:256] = source[0:512, 128:256] - a1 * (
            im[0:512, 128:256] - jnp.where(left, rolled[0:512], sign * roll64(got))
        )
        out[512:1024, 128:256] = source[512:1024, 128:256] - a1 * (
            im[512:1024, 128:256] - jnp.where(left, rolled[512:1024], sign * got)
        )
        return copy

    @pl.when(jnp.logical_not(has_below))
    def _():
        for ref in (sc1, sc2):
            ref[0:256, :] = jnp.zeros((256, 256), jnp.float32)
        for n in range(2):
            yr[n, 0] = jnp.zeros((256, 256), jnp.float32)

    @pl.when(jnp.logical_not(has_above))
    def _():
        for ref in (sc1, sc2):
            ref[1280:1536, :] = jnp.zeros((256, 256), jnp.float32)
        for n in range(2):
            yr[n, 1] = jnp.zeros((256, 256), jnp.float32)

    make_field(h)
    kown.wait()
    make_bands(h)
    c_px.wait_recv()
    t0 = swap_slices(d, slice(128, 256), 0, True)
    c_small.wait_recv()
    make_field(o)
    scaled_earlier(d, sc1, 0, t0)
    h0 = halo(sc1.at[256:512], sc1.at[1280:1536], sc1.at[1024:1280], sc1.at[0:256], 0)
    redsrc[0, 0:8] = squares(d)
    c_kx.wait_recv()
    got_k = kraw.at[pl.ds(o * 12 + t * 6, 6)]
    c_kc = remote(got_k, got_k, KC, mate)
    c_kc.start()
    c_kc.wait_recv()
    make_bands(o)
    halo_arrived(h0)
    vh[...], vl[...] = split(sc1[...])
    forward()
    redsrc[0, 8:16] = squares(im)
    reduce_start(0)
    b0 = backward(0)
    rr0, im_sum = reduce_done(0)
    alpha1 = rr0 / im_sum
    t1 = apply_later(0, b0, d, r1, alpha1)
    c_r1 = remote(r1.at[peer_rows], r1p, R1X, peer)
    t2 = swap_slices(r1, slice(128, 256), 2, True)
    redsrc[1, 0:8] = squares(r1)
    redsrc[1, 8:16] = jnp.zeros((8, 128), jnp.float32)
    reduce_start(1)
    scaled_earlier(r1, sc2, 2, t2)
    h1 = halo(sc2.at[256:512], sc2.at[1280:1536], sc2.at[1024:1280], sc2.at[0:256], 2)
    c_r1.start()

    rr1, _ = reduce_done(1)
    beta = rr1 / rr0
    beta2 = twice(beta)
    d[...] = r1[...] + beta2 * d[...]
    halo_arrived(h1)
    vh[...], vl[...] = split(sc2[...] + beta2 * sc1[...])
    forward()
    redsrc[2, 0:8] = squares(im)
    redsrc[2, 8:16] = jnp.zeros((8, 128), jnp.float32)
    reduce_start(2)
    halo_sent(b0)
    b1 = backward(1)
    im_sum, _ = reduce_done(2)
    alpha2 = rr1 / im_sum
    coef[0:8, :] = jnp.broadcast_to(alpha1 + alpha2 * beta, (8, 128))
    coef[8:16, :] = jnp.broadcast_to(alpha2, (8, 128))
    c_cx = remote(coef, coefp, CX, peer)
    c_cx.start()
    t3 = apply_later(1, b1, r1, r2, alpha2)
    c_r2 = remote(r2.at[peer_rows], r2p, R2X, peer)
    c_r2.start()

    def unpack(own, other):
        low = jnp.where(is0, own, other)
        high = jnp.where(is0, other, own)
        return jnp.where(left, low, roll64(high)), jnp.where(left, roll64(low), high)

    c_cx.wait_recv()
    c_r1.wait_recv()
    low_coef = jnp.where(is0, coef[...], coefp[...])
    high_coef = jnp.where(is0, coefp[...], coef[...])
    full = jnp.where(left, low_coef, high_coef)
    cp, cr = full[0:1], full[8:9]

    @pl.loop(0, 4)
    def _(i):
        rows = pl.ds(pl.multiple_of(i * B, B), B)
        mine_rows = pl.ds(pl.multiple_of(h * 512 + i * B, B), B)
        for a in range(2):
            cols = slice(a * 128, a * 128 + 128)
            va, vb = unpack(r1[mine_rows, cols], r1p[rows, cols])
            sol_ref[a, rows, :] = cp * x_ref[a, rows, :] + cr * va
            sol_ref[a + 2, rows, :] = cp * x_ref[a + 2, rows, :] + cr * vb

    c_r2.wait_recv()

    @pl.loop(0, 4)
    def _(i):
        rows = pl.ds(pl.multiple_of(i * B, B), B)
        mine_rows = pl.ds(pl.multiple_of(h * 512 + i * B, B), B)
        for a in range(2):
            cols = slice(a * 128, a * 128 + 128)
            va, vb = unpack(r2[mine_rows, cols], r2p[rows, cols])
            res_ref[a, rows, :] = va
            res_ref[a + 2, rows, :] = vb

    for copy in (c_px, c_small, c_kx, c_kc, t0, t1, t2, t3, c_r1, c_cx, c_r2):
        copy.wait_send()
    for copies in (h0, h1, b1):
        halo_sent(copies)
    for n in range(3):
        pltpu.make_async_copy(red.at[n], red.at[n], redss.at[n]).wait()


def local(probes, phi, kcols, kblocks):
    pairs = lax.axis_size("space") // 2
    own = kcols.shape[0]
    first = lax.axis_index("space") * own
    offset = kcols - (first + jnp.arange(own, dtype=jnp.int32))[:, None]
    chosen = offset[:, 1:, None] == jnp.array(OFFS, jnp.int32)[None, None, :]
    chosen = chosen.astype(jnp.float32).reshape(own, 8)
    chosen = jnp.broadcast_to(chosen[:, :, None], (own, 8, 128))
    angles = phi.reshape(4, own, B).transpose(1, 0, 2)
    angles = jnp.concatenate([angles, jnp.zeros_like(angles)], axis=1)
    small = jnp.concatenate([chosen, angles], axis=1).reshape(own * 16, 128)
    f32, bf16 = jnp.float32, jnp.bfloat16
    vmem = pl.BlockSpec(memory_space=pltpu.VMEM)
    team = 2 * pairs
    return pl.pallas_call(
        functools.partial(kernel, pairs),
        out_shape=[jax.ShapeDtypeStruct(probes.shape, f32)] * 2,
        in_specs=[vmem, vmem, pl.BlockSpec(memory_space=pl.ANY)],
        out_specs=[vmem, vmem],
        scratch_shapes=[
            pltpu.VMEM((512, 256), f32),
            pltpu.VMEM((1024, 256), f32),
            pltpu.VMEM((1024, 256), f32),
            pltpu.VMEM((1536, 256), f32),
            pltpu.VMEM((1536, 256), f32),
            pltpu.VMEM((1024, 256), f32),
            pltpu.VMEM((1536, 256), f32),
            pltpu.VMEM((1024, 256), f32),
            pltpu.VMEM((1024, 256), f32),
            pltpu.VMEM((512, 256), f32),
            pltpu.VMEM((512, 256), f32),
            pltpu.VMEM((2, 2, 256, 256), f32),
            pltpu.VMEM((4, 512, 128), f32),
            pltpu.VMEM((4, 512, 128), f32),
            pltpu.VMEM((2, 64, 128), f32),
            pltpu.VMEM((24, 128, 128), f32),
            pltpu.VMEM((4, 256, 768), bf16),
            pltpu.VMEM((4, 256, 768), bf16),
            pltpu.VMEM((4, 768, 256), bf16),
            pltpu.VMEM((4, 768, 256), bf16),
            pltpu.VMEM((1536, 256), bf16),
            pltpu.VMEM((1536, 256), bf16),
            pltpu.VMEM((3, 16, 128), f32),
            pltpu.VMEM((3, team - 1, 16, 128), f32),
            pltpu.VMEM((16, 128), f32),
            pltpu.VMEM((16, 128), f32),
            pltpu.SemaphoreType.DMA((NSEM,)),
            pltpu.SemaphoreType.DMA((NSEM,)),
            pltpu.SemaphoreType.DMA((3,)),
            pltpu.SemaphoreType.DMA((3,)),
            pltpu.SemaphoreType.DMA,
        ],
        compiler_params=pltpu.CompilerParams(
            collective_id=0, has_side_effects=True, vmem_limit_bytes=50 * 1024 * 1024
        ),
    )(probes, small, kblocks.reshape(own * 3, B, B))


def solution(mesh):
    panel = P(("groups", "tm"), "space", None)
    return jax.shard_map(
        local,
        mesh=mesh,
        in_specs=(
            panel, P(("groups", "tm"), "space"), P("space", None), P("space", None, None, None),
        ),
        out_specs=(panel, panel),
        check_vma=False,
    )
```

time: 269 us -> 86.3 us (0.32)
  blocking collectives: 93.3 us -> 0 us
  waiting for transfers between devices: 85.7 us -> 0 us
  Pallas kernels: 0 us -> 78.7 us
  matrix products: 29.6 us -> 0 us
  starting transfers between devices: 22.3 us -> 0 us
  local copies, waits for them, and re-layouts: 23.4 us -> 6.56 us
  other arithmetic: 12.8 us -> 0.15 us
    psum x3 -> x0, blocking collectives: 93.3 us -> none  [the longest x2 63.4 us: squares(): return lax.psum(column_sums(vector, vector), ('space', 'tm'))]
    ppermute x12 -> x0, waiting for transfers between devices: 85.7 us -> none  [the longest x2 42.8 us: padded(): before = lax.ppermute(last, axis, up)]
    pallas_call x0 -> x1, Pallas kernels: none -> 78.7 us  [local(): pl.pallas_call(functools.partial(kernel, pairs), out_shape=[jax.ShapeDtyp...]
    dot_general x6 -> x0, matrix products: 29.6 us -> none  [the longest x2 12.1 us: local(): jnp.einsum('cm,scap->smap', spread_onehot, terms, precision=highest)]
    ppermute x12 -> x0, starting transfers between devices: 22.3 us -> none  [the longest x4 12.9 us: from_behind(): return lax.ppermute(block, axis, route)]
    transpose x4 -> x0, local copies, waits for them, and re-layouts: 7.27 us -> none  [the longest x2 7.13 us: local(): terms = jnp.einsum('nkba,snbp->snkap', kblocks, pieces, precision=highest)]
    gather x2 -> x0, local copies, waits for them, and re-layouts: 6.35 us -> none  [local(): picked = jnp.take(forward_pieces, local_cols, axis=1)]
    slice x11 -> x1, local copies, waits for them, and re-layouts: 3.67 us -> 0.07 us  [local(): chosen = offset[:, 1:, None] == jnp.array(OFFS, jnp.int32)[None, None, :]]
  transfers between devices with their start and end apart: 12 -> 0, of which waited for: 8 -> 0; matrix products, arithmetic and copies ran while one was open for 2% -> 0% of each run, Pallas kernels for 0% -> 0%
where the time goes in v1:
time: 86.3 us; the launch traced here: 86.1 us
  Pallas kernels  78.7 us (91%)
  local copies, waits for them, and re-layouts  6.56 us (8%)
    pallas_call x1, Pallas kernels, local(): pl.pallas_call(functools.partial(kernel, pairs), out_shape=[jax.ShapeDtyp...  78.7 us
    unnamed x12, local copies, waits for them, and re-layouts  6.1 us

profile of v1, /device:TPU:0, one launch (start us, length us, event | category | flops | bytes accessed | tf_op | source)
XLA Modules:
  0.0 86.1 jit_solution(6172915164541350990)
XLA Ops:
  0.7 0.0 copy-start.4
  0.7 0.1 pad.2.clone
  0.7 0.6 copy-done.4
  1.3 0.0 copy-start.3
  1.3 0.1 eq.26
  1.4 0.6 copy-done.3
  2.0 0.1 broadcast_subtract_fusion
  2.1 0.1 slice.3
  2.1 0.1 eq.23
  2.2 0.1 eq.24
  2.3 0.0 copy-start.2
  2.3 0.1 broadcast_in_dim.4
  2.4 0.6 copy-done.2
  3.0 0.1 maximum_maximum_fusion
  3.1 0.0 copy-start
  3.1 1.2 %copy-done = f32[4,512,128]{2,1,0:T(8,128)S(1)} copy-done((f32[4,512,128]{2,1,0:T(8,128)S(1)}, f32[4,512,128]{2,1,0:T(8,128)}, u32[]{:S(2)}) %copy-start) | copy-done | bytes 1048600
  4.3 0.0 copy-start.1
  4.3 1.1 %copy-done.1 = f32[4,3,128,128]{3,2,1,0:T(8,128)S(1)} copy-done((f32[4,3,128,128]{3,2,1,0:T(8,128)S(1)}, f32[4,3,128,128]{3,2,1,0:T(8,128)}, u32[]{:S(2)}) %copy-start.1) | copy-done | bytes 786456
  5.4 78.7 %shard_map.68 = (f32[4,512,128]{2,1,0:T(8,128)S(1)}, f32[4,512,128]{2,1,0:T(8,128)S(1)}) custom-call(f32[4,512,128]{2,1,0:T(8,128)S(1)} %copy-done, f32[64,128]{1,0:T(8,128)S(1)} %bitcast.6, f32[12,128,128]{2,1,0:T(8,128)S(1)} %bitcast.5), custom_call_target="tpu_custom_call" | custom-call | tf_op jit(solution)/shard_map/pallas_call | solution.py:397
  84.1 1.0 %copy.10 = f32[4,512,128]{2,1,0:T(8,128)} copy(f32[4,512,128]{2,1,0:T(8,128)S(1)} %get-tuple-element.4) | data formatting | bytes 2097152
  85.1 1.0 %copy.11 = f32[4,512,128]{2,1,0:T(8,128)} copy(f32[4,512,128]{2,1,0:T(8,128)S(1)} %get-tuple-element.5) | data formatting | bytes 2097152
  (4 shorter events, 0.0 us)
Async XLA Ops:
  0.7 0.7 copy-start.4
  1.3 0.7 copy-start.3
  2.3 0.7 copy-start.2
  3.1 1.2 %copy-start = (f32[4,512,128]{2,1,0:T(8,128)S(1)}, f32[4,512,128]{2,1,0:T(8,128)}, u32[]{:S(2)}) copy-start(f32[4,512,128]{2,1,0:T(8,128)} %x_ref.1) | copy-start | bytes 3145732
  4.3 1.1 %copy-start.1 = (f32[4,3,128,128]{3,2,1,0:T(8,128)S(1)}, f32[4,3,128,128]{3,2,1,0:T(8,128)}, u32[]{:S(2)}) copy-start(f32[4,3,128,128]{3,2,1,0:T(8,128)} %param.8) | copy-start | bytes 2359300

commit v2 on v1

--- a/solution.py
+++ b/solution.py
@@ -12,8 +12,11 @@
 OFFS = (-2, -1, 1, 2)
 
 
-PX, SMALL, KX, KC, TM, DOWN, UP, R1X, R2X, CX = 0, 1, 2, 3, 4, 8, 12, 16, 17, 18
-NSEM = 19
+SMALL, KX, KY, KC, KD, R1X, CX, PX, R2X, DOWN, UP, TM = 0, 1, 2, 3, 4, 5, 6, 7, 9, 11, 15, 19
+NSEM = 27
+
+RIM, INNER = 0, 1
+RUNS = (((0, 256), (768, 1024)), ((256, 512), (512, 768)))
 
 
 def roll64(x):
@@ -30,10 +33,10 @@
 
 
 def kernel(
-    pairs, x_ref, small_ref, k_ref, sol_ref, res_ref,
-    px, d, f, sc1, sc2, im, y, r1, r2, r1p, r2p, yr, tms, tmr, smalls, kraw,
+    pairs, x_hbm, phi_ref, cols_ref, k_ref, sol_ref, res_ref,
+    x_ref, px, d, f, sc1, sc2, im, y, r1, r2, r1p, r2p, yr, tms, tmr, smalls, kraw,
     kh, kl, kth, ktl, vh, vl, redsrc, red, coef, coefp,
-    ssem, rsem, redss, redrs, lsem,
+    ssem, rsem, redss, redrs, lsem, xsem,
 ):
     g, s, t = lax.axis_index("groups"), lax.axis_index("space"), lax.axis_index("tm")
     p, h = s // 2, s % 2
@@ -42,6 +45,7 @@
     me = p * 2 + t
     peer = (g, s + 1 - 2 * h, t)
     mate = (g, s, 1 - t)
+    twin = (1 - g, s, t)
     below = (g, jnp.maximum(s - 2, 0), t)
     above = (g, jnp.minimum(s + 2, 2 * pairs - 1), t)
     has_below, has_above = p > 0, p < pairs - 1
@@ -58,6 +62,9 @@
         )
 
     pl.semaphore_signal(barrier, inc=1, device_id=peer, device_id_type=MESH)
+    pl.semaphore_signal(barrier, inc=1, device_id=twin, device_id_type=MESH)
+    xload = pltpu.make_async_copy(x_hbm, x_ref, xsem)
+    xload.start()
 
     lane = lax.broadcasted_iota(jnp.int32, (1, 128), 1)
     left = lane < 64
@@ -69,10 +76,39 @@
             device_id=device, device_id_type=MESH,
         )
 
-    own_rows = pl.ds(pl.multiple_of(h * 512, 512), 512)
     peer_rows = pl.ds(pl.multiple_of(o * 512, 512), 512)
+    part_rows = (
+        pl.ds(pl.multiple_of(o * 768, 256), 256),
+        pl.ds(pl.multiple_of(256 + o * 256, 256), 256),
+    )
+    part_at = (
+        pl.ds(pl.multiple_of(o * 256, 256), 256),
+        pl.ds(pl.multiple_of(h * 256, 256), 256),
+    )
+    own_part_rows = (
+        pl.ds(pl.multiple_of(h * 768, 256), 256),
+        pl.ds(pl.multiple_of(256 + h * 256, 256), 256),
+    )
+    own_part_at = (
+        pl.ds(pl.multiple_of(h * 256, 256), 256),
+        pl.ds(pl.multiple_of(o * 256, 256), 256),
+    )
     kown = pltpu.make_async_copy(k_ref, kraw.at[pl.ds(h * 12, 12)], lsem)
     kown.start()
+
+    sub = lax.broadcasted_iota(jnp.int32, (8, 128), 0)
+    for j in range(4):
+        chosen = jnp.zeros((8, 128), jnp.float32)
+        for k in range(2):
+            distance = cols_ref[j, 1 + k] - (s * 4 + j)
+            for i1, off in enumerate(OFFS):
+                hit = jnp.where(distance == off, 1.0, 0.0)
+                chosen = jnp.where(sub == 4 * k + i1, hit, chosen)
+        smalls[h, j * 16 : j * 16 + 8, :] = chosen
+        part = phi_ref[:, j * B : j * B + B]
+        smalls[h, j * 16 + 8 : j * 16 + 16, :] = jnp.concatenate([part, part], axis=0)
+
+    xload.wait()
 
     @pl.loop(0, 4)
     def _(i):
@@ -86,15 +122,19 @@
             px[rows, cols] = jnp.where(is0, high, low)
             d[mine_rows, cols] = jnp.where(is0, low, high)
 
-    smalls[h] = small_ref[...]
-    pl.semaphore_wait(barrier, team)
-
-    c_px = remote(px, d.at[own_rows], PX, peer)
-    c_px.start()
-    c_small = remote(small_ref, smalls.at[h], SMALL, peer)
+    pl.semaphore_wait(barrier, team + 1)
+
+    c_small = remote(smalls.at[h], smalls.at[h], SMALL, peer)
     c_small.start()
-    c_kx = remote(k_ref.at[pl.ds(t * 6, 6)], kraw.at[pl.ds(h * 12 + t * 6, 6)], KX, peer)
+    c_px = [
+        remote(px.at[own_part_at[n]], d.at[own_part_rows[n]], PX + n, peer) for n in range(2)
+    ]
+    c_px[RIM].start()
+    row = g * 2 + t
+    sent_k = pl.ds(h * 12 + row * 3, 3)
+    c_kx = remote(k_ref.at[pl.ds(row * 3, 3)], kraw.at[sent_k], KX, peer)
     c_kx.start()
+    c_px[INNER].start()
 
     def make_field(half):
         @pl.loop(0, 4)
@@ -135,13 +175,15 @@
                     kh[band, rr, wc], kl[band, rr, wc] = split(blk)
                     kth[band, wc, rr], ktl[band, wc, rr] = split(blt)
 
-    def swap_slices(panel, cols, n, first_half_rolled):
-        a, b = panel[0:512, cols], panel[512:1024, cols]
+    def swap_part(panel, cols, n, first_half_rolled, part):
+        (a0, a1), (b0, b1) = RUNS[part]
+        a, b = panel[a0:a1, cols], panel[b0:b1, cols]
+        rows = slice(part * 256, part * 256 + 256)
         if first_half_rolled:
-            tms[n] = jnp.where(left, roll64(a), b)
+            tms[n, rows] = jnp.where(left, roll64(a), b)
         else:
-            tms[n] = jnp.where(left, a, roll64(b))
-        copy = remote(tms.at[n], tmr.at[n], TM + n, mate)
+            tms[n, rows] = jnp.where(left, a, roll64(b))
+        copy = remote(tms.at[n, rows], tmr.at[n, rows], TM + 2 * n + part, mate)
         copy.start()
         return copy
 
@@ -181,16 +223,16 @@
         def _():
             up.wait_send()
 
-    def scaled_earlier(panel, out, n, copy):
+    def scaled_part(panel, out, n, copy, part):
         copy.wait_recv()
         sign = jnp.where(t == 0, -1.0, 1.0)
-        got = tmr[n]
-        rolled = roll64(panel[:, 128:256])
-        out[256:768, 0:128] = f[0:512, 0:128] * jnp.where(left, sign * got, rolled[0:512])
-        out[768:1280, 0:128] = f[512:1024, 0:128] * jnp.where(
-            left, sign * roll64(got), rolled[512:1024]
-        )
-        out[256:1280, 128:256] = f[:, 128:256] * panel[:, 0:128]
+        got = tmr[n, part * 256 : part * 256 + 256]
+        for (b0, b1), from_mate in zip(RUNS[part], (got, roll64(got))):
+            q0, q1 = b0 + 256, b1 + 256
+            out[q0:q1, 0:128] = f[b0:b1, 0:128] * jnp.where(
+                left, sign * from_mate, roll64(panel[b0:b1, 128:256])
+            )
+            out[q0:q1, 128:256] = f[b0:b1, 128:256] * panel[b0:b1, 0:128]
 
     def squares(panel):
         q = panel[...]
@@ -218,20 +260,33 @@
     def twice(v):
         return jnp.concatenate([v, v], axis=1)
 
-    def forward():
-        @pl.loop(0, 4)
+    def forward_rows(i):
+        win = pl.ds(pl.multiple_of(i * 256, 256), 768)
+        rows = pl.ds(pl.multiple_of(i * 256, 256), 256)
+        vhi = vh[win, :]
+        acc = dot(kh[i], vhi) + dot(kl[i], vhi) + dot(kh[i], vl[win, :])
+        im[rows, :] = d[rows, :] - acc
+
+    def forward(value, copies):
+        vh[256:1280, :], vl[256:1280, :] = split(value(256, 1280))
+
+        @pl.loop(1, 3)
         def _(i):
-            win = pl.ds(pl.multiple_of(i * 256, 256), 768)
-            rows = pl.ds(pl.multiple_of(i * 256, 256), 256)
-            vhi = vh[win, :]
-            acc = dot(kh[i], vhi) + dot(kl[i], vhi) + dot(kh[i], vl[win, :])
-            im[rows, :] = d[rows, :] - acc
+            forward_rows(i)
+
+        halo_arrived(copies)
+        vh[0:256, :], vl[0:256, :] = split(value(0, 256))
+        vh[1280:1536, :], vl[1280:1536, :] = split(value(1280, 1536))
+
+        @pl.loop(0, 2)
+        def _(i):
+            forward_rows(i * 3)
 
     def back_part(i):
         zh, zl = split(im[pl.ds(pl.multiple_of(i * 256, 256), 256), :])
         return dot(kth[i], zh) + dot(ktl[i], zh) + dot(kth[i], zl)
 
-    def backward(n):
+    def backward(n, round_of):
         @pl.loop(0, 2)
         def _(i):
             y[pl.ds(pl.multiple_of(i * 768, 256), 768), :] = back_part(i * 3)
@@ -239,6 +294,9 @@
         copies = halo(
             y.at[0:256], yr.at[n, 1], y.at[1280:1536], yr.at[n, 0], 1 + 2 * n
         )
+
+        redsrc[round_of, 8:16] = squares(im)
+        reduce_start(round_of)
 
         @pl.loop(1, 3)
         def _(i):
@@ -247,26 +305,23 @@
 
         return copies
 
-    def apply_later(n, copies, source, out, alpha):
-        halo_arrived(copies)
-        y[256:512, :] = f[0:256, :] * (y[256:512, :] + yr[n, 0])
-        y[512:1024, :] = f[256:768, :] * y[512:1024, :]
-        y[1024:1280, :] = f[768:1024, :] * (y[1024:1280, :] + yr[n, 1])
-        slot = 1 + 2 * n
-        copy = swap_slices(y.at[256:1280], slice(0, 128), slot, False)
-        a1 = alpha
-        out[:, 0:128] = source[:, 0:128] - a1 * (im[:, 0:128] - y[256:1280, 128:256])
+    def scale_back(n, part):
+        for side, (b0, b1) in enumerate(RUNS[part]):
+            got = y[b0 + 256 : b1 + 256, :]
+            if part == RIM:
+                got = got + yr[n, side]
+            y[b0 + 256 : b1 + 256, :] = f[b0:b1, :] * got
+        return swap_part(y.at[256:1280], slice(0, 128), 1 + 2 * n, False, part)
+
+    def apply_part(n, copy, source, out, alpha, part):
         copy.wait_recv()
         sign = jnp.where(t == 1, -1.0, 1.0)
-        got = tmr[slot]
-        rolled = roll64(y[256:1280, 0:128])
-        out[0:512, 128:256] = source[0:512, 128:256] - a1 * (
-            im[0:512, 128:256] - jnp.where(left, rolled[0:512], sign * roll64(got))
-        )
-        out[512:1024, 128:256] = source[512:1024, 128:256] - a1 * (
-            im[512:1024, 128:256] - jnp.where(left, rolled[512:1024], sign * got)
-        )
-        return copy
+        got = tmr[1 + 2 * n, part * 256 : part * 256 + 256]
+        for (b0, b1), from_mate in zip(RUNS[part], (roll64(got), got)):
+            g0, g1 = y[b0 + 256 : b1 + 256, 0:128], y[b0 + 256 : b1 + 256, 128:256]
+            later = jnp.where(left, roll64(g0), sign * from_mate)
+            out[b0:b1, 0:128] = source[b0:b1, 0:128] - alpha * (im[b0:b1, 0:128] - g1)
+            out[b0:b1, 128:256] = source[b0:b1, 128:256] - alpha * (im[b0:b1, 128:256] - later)
 
     @pl.when(jnp.logical_not(has_below))
     def _():
@@ -282,61 +337,80 @@
         for n in range(2):
             yr[n, 1] = jnp.zeros((256, 256), jnp.float32)
 
+    swapped = []
+    last = slice(128, 256)
     make_field(h)
     kown.wait()
     make_bands(h)
-    c_px.wait_recv()
-    t0 = swap_slices(d, slice(128, 256), 0, True)
+    c_px[RIM].wait_recv()
+    rim = swap_part(d, last, 0, True, RIM)
     c_small.wait_recv()
     make_field(o)
-    scaled_earlier(d, sc1, 0, t0)
+    c_kx.wait_recv()
+    first_k = kraw.at[pl.ds(o * 12 + row * 3, 3)]
+    c_ky = remote(first_k, first_k, KY, twin)
+    c_ky.start()
+    c_kc = remote(first_k, first_k, KC, mate)
+    c_kc.start()
+    scaled_part(d, sc1, 0, rim, RIM)
     h0 = halo(sc1.at[256:512], sc1.at[1280:1536], sc1.at[1024:1280], sc1.at[0:256], 0)
+    c_px[INNER].wait_recv()
+    inner = swap_part(d, last, 0, True, INNER)
+    swapped += [rim, inner]
     redsrc[0, 0:8] = squares(d)
-    c_kx.wait_recv()
-    got_k = kraw.at[pl.ds(o * 12 + t * 6, 6)]
-    c_kc = remote(got_k, got_k, KC, mate)
-    c_kc.start()
+    c_ky.wait_recv()
+    other_k = kraw.at[pl.ds(o * 12 + ((1 - g) * 2 + t) * 3, 3)]
+    c_kd = remote(other_k, other_k, KD, mate)
+    c_kd.start()
+    scaled_part(d, sc1, 0, inner, INNER)
     c_kc.wait_recv()
+    c_kd.wait_recv()
     make_bands(o)
-    halo_arrived(h0)
-    vh[...], vl[...] = split(sc1[...])
-    forward()
-    redsrc[0, 8:16] = squares(im)
-    reduce_start(0)
-    b0 = backward(0)
+    forward(lambda a, b: sc1[a:b, :], h0)
+    b0 = backward(0, 0)
+    inner = scale_back(0, INNER)
     rr0, im_sum = reduce_done(0)
     alpha1 = rr0 / im_sum
-    t1 = apply_later(0, b0, d, r1, alpha1)
-    c_r1 = remote(r1.at[peer_rows], r1p, R1X, peer)
-    t2 = swap_slices(r1, slice(128, 256), 2, True)
+    alpha = alpha1
+    apply_part(0, inner, d, r1, alpha, INNER)
+    next_inner = swap_part(r1, last, 2, True, INNER)
+    halo_arrived(b0)
+    rim = scale_back(0, RIM)
+    apply_part(0, rim, d, r1, alpha, RIM)
+    next_rim = swap_part(r1, last, 2, True, RIM)
+    swapped += [inner, rim, next_inner, next_rim]
     redsrc[1, 0:8] = squares(r1)
     redsrc[1, 8:16] = jnp.zeros((8, 128), jnp.float32)
     reduce_start(1)
-    scaled_earlier(r1, sc2, 2, t2)
+    scaled_part(r1, sc2, 2, next_rim, RIM)
     h1 = halo(sc2.at[256:512], sc2.at[1280:1536], sc2.at[1024:1280], sc2.at[0:256], 2)
+    c_r1 = remote(r1.at[peer_rows], r1p, R1X, peer)
     c_r1.start()
-
+    scaled_part(r1, sc2, 2, next_inner, INNER)
+
+    redsrc[2, 0:8] = jnp.zeros((8, 128), jnp.float32)
     rr1, _ = reduce_done(1)
     beta = rr1 / rr0
     beta2 = twice(beta)
     d[...] = r1[...] + beta2 * d[...]
-    halo_arrived(h1)
-    vh[...], vl[...] = split(sc2[...] + beta2 * sc1[...])
-    forward()
-    redsrc[2, 0:8] = squares(im)
-    redsrc[2, 8:16] = jnp.zeros((8, 128), jnp.float32)
-    reduce_start(2)
+    forward(lambda a, b: sc2[a:b, :] + beta2 * sc1[a:b, :], h1)
     halo_sent(b0)
-    b1 = backward(1)
-    im_sum, _ = reduce_done(2)
+    b1 = backward(1, 2)
+    inner = scale_back(1, INNER)
+    _, im_sum = reduce_done(2)
     alpha2 = rr1 / im_sum
     coef[0:8, :] = jnp.broadcast_to(alpha1 + alpha2 * beta, (8, 128))
     coef[8:16, :] = jnp.broadcast_to(alpha2, (8, 128))
     c_cx = remote(coef, coefp, CX, peer)
     c_cx.start()
-    t3 = apply_later(1, b1, r1, r2, alpha2)
-    c_r2 = remote(r2.at[peer_rows], r2p, R2X, peer)
-    c_r2.start()
+    apply_part(1, inner, r1, r2, alpha2, INNER)
+    c_r2 = [remote(r2.at[part_rows[n]], r2p.at[part_at[n]], R2X + n, peer) for n in range(2)]
+    c_r2[INNER].start()
+    halo_arrived(b1)
+    rim = scale_back(1, RIM)
+    apply_part(1, rim, r1, r2, alpha2, RIM)
+    c_r2[RIM].start()
+    swapped += [inner, rim]
 
     def unpack(own, other):
         low = jnp.where(is0, own, other)
@@ -360,19 +434,19 @@
             sol_ref[a, rows, :] = cp * x_ref[a, rows, :] + cr * va
             sol_ref[a + 2, rows, :] = cp * x_ref[a + 2, rows, :] + cr * vb
 
-    c_r2.wait_recv()
-
-    @pl.loop(0, 4)
-    def _(i):
-        rows = pl.ds(pl.multiple_of(i * B, B), B)
-        mine_rows = pl.ds(pl.multiple_of(h * 512 + i * B, B), B)
-        for a in range(2):
-            cols = slice(a * 128, a * 128 + 128)
-            va, vb = unpack(r2[mine_rows, cols], r2p[rows, cols])
-            res_ref[a, rows, :] = va
-            res_ref[a + 2, rows, :] = vb
-
-    for copy in (c_px, c_small, c_kx, c_kc, t0, t1, t2, t3, c_r1, c_cx, c_r2):
+    for part in (INNER, RIM):
+        c_r2[part].wait_recv()
+        for i in range(2):
+            start = h * 256 if part == RIM else o * 256
+            rows = pl.ds(pl.multiple_of(start + i * B, B), B)
+            mine_rows = pl.ds(pl.multiple_of(h * 512 + start + i * B, B), B)
+            for a in range(2):
+                cols = slice(a * 128, a * 128 + 128)
+                va, vb = unpack(r2[mine_rows, cols], r2p[rows, cols])
+                res_ref[a, rows, :] = va
+                res_ref[a + 2, rows, :] = vb
+
+    for copy in [*c_px, c_small, c_kx, c_ky, c_kc, c_kd, *swapped, c_r1, c_cx, *c_r2]:
         copy.wait_send()
     for copies in (h0, h1, b1):
         halo_sent(copies)
@@ -383,23 +457,19 @@
 def local(probes, phi, kcols, kblocks):
     pairs = lax.axis_size("space") // 2
     own = kcols.shape[0]
-    first = lax.axis_index("space") * own
-    offset = kcols - (first + jnp.arange(own, dtype=jnp.int32))[:, None]
-    chosen = offset[:, 1:, None] == jnp.array(OFFS, jnp.int32)[None, None, :]
-    chosen = chosen.astype(jnp.float32).reshape(own, 8)
-    chosen = jnp.broadcast_to(chosen[:, :, None], (own, 8, 128))
-    angles = phi.reshape(4, own, B).transpose(1, 0, 2)
-    angles = jnp.concatenate([angles, jnp.zeros_like(angles)], axis=1)
-    small = jnp.concatenate([chosen, angles], axis=1).reshape(own * 16, 128)
     f32, bf16 = jnp.float32, jnp.bfloat16
     vmem = pl.BlockSpec(memory_space=pltpu.VMEM)
     team = 2 * pairs
     return pl.pallas_call(
         functools.partial(kernel, pairs),
         out_shape=[jax.ShapeDtypeStruct(probes.shape, f32)] * 2,
-        in_specs=[vmem, vmem, pl.BlockSpec(memory_space=pl.ANY)],
+        in_specs=[
+            pl.BlockSpec(memory_space=pl.ANY), vmem,
+            pl.BlockSpec(memory_space=pltpu.SMEM), pl.BlockSpec(memory_space=pl.ANY),
+        ],
         out_specs=[vmem, vmem],
         scratch_shapes=[
+            pltpu.VMEM((4, 512, 128), f32),
             pltpu.VMEM((512, 256), f32),
             pltpu.VMEM((1024, 256), f32),
             pltpu.VMEM((1024, 256), f32),
@@ -431,11 +501,12 @@
             pltpu.SemaphoreType.DMA((3,)),
             pltpu.SemaphoreType.DMA((3,)),
             pltpu.SemaphoreType.DMA,
+            pltpu.SemaphoreType.DMA,
         ],
         compiler_params=pltpu.CompilerParams(
-            collective_id=0, has_side_effects=True, vmem_limit_bytes=50 * 1024 * 1024
+            collective_id=0, has_side_effects=True, vmem_limit_bytes=60 * 1024 * 1024
         ),
-    )(probes, small, kblocks.reshape(own * 3, B, B))
+    )(probes, phi, kcols, kblocks.reshape(own * 3, B, B))
 
 
 def solution(mesh):

time: 86.3 us -> 80.3 us (0.930)
  local copies, waits for them, and re-layouts: 6.56 us -> 3.32 us
  Pallas kernels: 78.7 us -> 76.1 us
    unnamed x12 -> x4, local copies, waits for them, and re-layouts: 6.1 us -> 3.32 us
    pallas_call x1, Pallas kernels: 78.7 us -> 76.1 us  [local(): pl.pallas_call(functools.partial(kernel, pairs), out_shape=[jax.ShapeDtyp...]
where the time goes in v2:
time: 80.3 us; the launch traced here: 80.1 us
  Pallas kernels  76.1 us (95%)
  local copies, waits for them, and re-layouts  3.32 us (4%)
    pallas_call x1, Pallas kernels, local(): pl.pallas_call(functools.partial(kernel, pairs), out_shape=[jax.ShapeDtyp...  76.1 us
    unnamed x4, local copies, waits for them, and re-layouts  3.32 us

profile of v2, /device:TPU:0, one launch (start us, length us, event | category | flops | bytes accessed | tf_op | source)
XLA Modules:
  0.0 80.1 jit_solution(16846528060525568586)
XLA Ops:
  0.6 76.1 %shard_map.59 = (f32[4,512,128]{2,1,0:T(8,128)}, f32[4,512,128]{2,1,0:T(8,128)}) custom-call(f32[4,512,128]{2,1,0:T(8,128)} %x_hbm.1, f32[4,512]{1,0:T(4,128)} %phi_ref.1, s32[4,3]{1,0:T(4,128)} %cols_ref.1, f32[12,128,128]{2,1,0:T(8,128)} %bitcast.1), custom_call_target="tpu_custom_call" | custom-call | tf_op jit(solution)/shard_map/pallas_call | solution.py:463
  76.7 0.0 copy-start
  76.7 2.4 %copy.8 = f32[4,512,128]{2,1,0:T(8,128)} copy(f32[4,512,128]{2,1,0:T(8,128)} %get-tuple-element.4) | data formatting | bytes 2097152
  79.1 0.0 copy-done
  79.1 1.0 %copy.9 = f32[4,512,128]{2,1,0:T(8,128)} copy(f32[4,512,128]{2,1,0:T(8,128)S(1)} %copy-done) | data formatting | bytes 2097152
Async XLA Ops:
  76.7 2.4 %copy-start = (f32[4,512,128]{2,1,0:T(8,128)S(1)}, f32[4,512,128]{2,1,0:T(8,128)}, u32[]{:S(2)}) copy-start(f32[4,512,128]{2,1,0:T(8,128)} %get-tuple-element.5) | copy-start | bytes 3145732

commit v3 on v2

--- a/solution.py
+++ b/solution.py
@@ -12,8 +12,8 @@
 OFFS = (-2, -1, 1, 2)
 
 
-SMALL, KX, KY, KC, KD, R1X, CX, PX, R2X, DOWN, UP, TM = 0, 1, 2, 3, 4, 5, 6, 7, 9, 11, 15, 19
-NSEM = 27
+SMALL, KX, KY, KC, KD, CX, PX, R1X, R2X, DOWN, UP, TM = 0, 1, 2, 3, 4, 5, 6, 8, 10, 12, 16, 20
+NSEM = 28
 
 RIM, INNER = 0, 1
 RUNS = (((0, 256), (768, 1024)), ((256, 512), (512, 768)))
@@ -76,7 +76,6 @@
             device_id=device, device_id_type=MESH,
         )
 
-    peer_rows = pl.ds(pl.multiple_of(o * 512, 512), 512)
     part_rows = (
         pl.ds(pl.multiple_of(o * 768, 256), 256),
         pl.ds(pl.multiple_of(256 + o * 256, 256), 256),
@@ -374,18 +373,19 @@
     alpha = alpha1
     apply_part(0, inner, d, r1, alpha, INNER)
     next_inner = swap_part(r1, last, 2, True, INNER)
+    c_r1 = [remote(r1.at[part_rows[n]], r1p.at[part_at[n]], R1X + n, peer) for n in range(2)]
+    c_r1[INNER].start()
     halo_arrived(b0)
     rim = scale_back(0, RIM)
     apply_part(0, rim, d, r1, alpha, RIM)
     next_rim = swap_part(r1, last, 2, True, RIM)
+    c_r1[RIM].start()
     swapped += [inner, rim, next_inner, next_rim]
     redsrc[1, 0:8] = squares(r1)
     redsrc[1, 8:16] = jnp.zeros((8, 128), jnp.float32)
     reduce_start(1)
     scaled_part(r1, sc2, 2, next_rim, RIM)
     h1 = halo(sc2.at[256:512], sc2.at[1280:1536], sc2.at[1024:1280], sc2.at[0:256], 2)
-    c_r1 = remote(r1.at[peer_rows], r1p, R1X, peer)
-    c_r1.start()
     scaled_part(r1, sc2, 2, next_inner, INNER)
 
     redsrc[2, 0:8] = jnp.zeros((8, 128), jnp.float32)
@@ -418,7 +418,8 @@
         return jnp.where(left, low, roll64(high)), jnp.where(left, roll64(low), high)
 
     c_cx.wait_recv()
-    c_r1.wait_recv()
+    c_r1[INNER].wait_recv()
+    c_r1[RIM].wait_recv()
     low_coef = jnp.where(is0, coef[...], coefp[...])
     high_coef = jnp.where(is0, coefp[...], coef[...])
     full = jnp.where(left, low_coef, high_coef)
@@ -446,7 +447,7 @@
                 res_ref[a, rows, :] = va
                 res_ref[a + 2, rows, :] = vb
 
-    for copy in [*c_px, c_small, c_kx, c_ky, c_kc, c_kd, *swapped, c_r1, c_cx, *c_r2]:
+    for copy in [*c_px, c_small, c_kx, c_ky, c_kc, c_kd, *swapped, *c_r1, c_cx, *c_r2]:
         copy.wait_send()
     for copies in (h0, h1, b1):
         halo_sent(copies)
@@ -504,7 +505,7 @@
             pltpu.SemaphoreType.DMA,
         ],
         compiler_params=pltpu.CompilerParams(
-            collective_id=0, has_side_effects=True, vmem_limit_bytes=60 * 1024 * 1024
+            collective_id=0, has_side_effects=True, vmem_limit_bytes=54 * 1024 * 1024
         ),
     )(probes, phi, kcols, kblocks.reshape(own * 3, B, B))
 

time: 80.3 us -> 80.3 us (level)
  no operation moved by 1% of the time
where the time goes in v3:
time: 80.3 us; the launch traced here: 80.1 us
  Pallas kernels  76.1 us (95%)
  local copies, waits for them, and re-layouts  3.32 us (4%)
    pallas_call x1, Pallas kernels, local(): pl.pallas_call(functools.partial(kernel, pairs), out_shape=[jax.ShapeDtyp...  76.1 us
    unnamed x4, local copies, waits for them, and re-layouts  3.32 us

profile of v3, /device:TPU:0, one launch (start us, length us, event | category | flops | bytes accessed | tf_op | source)
XLA Modules:
  0.0 80.1 jit_solution(90486354653688576)
XLA Ops:
  0.6 76.1 %shard_map.59 = (f32[4,512,128]{2,1,0:T(8,128)}, f32[4,512,128]{2,1,0:T(8,128)}) custom-call(f32[4,512,128]{2,1,0:T(8,128)} %x_hbm.1, f32[4,512]{1,0:T(4,128)} %phi_ref.1, s32[4,3]{1,0:T(4,128)} %cols_ref.1, f32[12,128,128]{2,1,0:T(8,128)} %bitcast.1), custom_call_target="tpu_custom_call" | custom-call | tf_op jit(solution)/shard_map/pallas_call | solution.py:464
  76.8 0.0 copy-start
  76.8 2.4 %copy.8 = f32[4,512,128]{2,1,0:T(8,128)} copy(f32[4,512,128]{2,1,0:T(8,128)} %get-tuple-element.4) | data formatting | bytes 2097152
  79.1 0.0 copy-done
  79.1 1.0 %copy.9 = f32[4,512,128]{2,1,0:T(8,128)} copy(f32[4,512,128]{2,1,0:T(8,128)S(1)} %copy-done) | data formatting | bytes 2097152
Async XLA Ops:
  76.8 2.4 %copy-start = (f32[4,512,128]{2,1,0:T(8,128)S(1)}, f32[4,512,128]{2,1,0:T(8,128)}, u32[]{:S(2)}) copy-start(f32[4,512,128]{2,1,0:T(8,128)} %get-tuple-element.5) | copy-start | bytes 3145732
